TPU v7x, 32 devices: a whole 2x2x4 slice. The times are simulated.
32 devices in a mesh: expert: 4 (over z), hidden: 2 (over core), dp: 4 (over y, x).
Axes of the slice: x: 2, y: 2, z: 4, core: 2. Of those that a mesh axis runs over, the one named last changes fastest.
Arguments:
- tokens: bfloat16 [20480, 768], P(('expert', 'hidden', 'dp')), may hold values from -6 to 6
- cotangent: bfloat16 [20480, 768], P(('expert', 'hidden', 'dp')), may hold values from -6 to 6
- ln1_gain: float32 [768], replicated, may hold values from 0.5 to 1.5
- ln1_shift: float32 [768], replicated, may hold values from -1.5 to 1.5
- w_query: bfloat16 [768, 768], replicated, may hold values from -0.21875 to 0.21875
- w_key: bfloat16 [768, 768], replicated, may hold values from -0.21875 to 0.21875
- w_value: bfloat16 [768, 768], replicated, may hold values from -0.21875 to 0.21875
- w_output: bfloat16 [768, 768], replicated, may hold values from -1.75 to 1.75
- ln2_gain: float32 [768], replicated, may hold values from 0.5 to 1.5
- ln2_shift: float32 [768], replicated, may hold values from -1.5 to 1.5
- w_router: bfloat16 [768, 4], replicated, may hold values from -0.15625 to 0.15625
- w_inner: bfloat16 [4, 768, 3072], P('expert', None, 'hidden'), may hold values from -0.21875 to 0.21875
- b_inner: bfloat16 [4, 3072], P('expert', 'hidden'), may hold values from -0.59765625 to 0.59765625
- w_outer: bfloat16 [4, 3072, 768], P('expert', 'hidden'), may hold values from -1.75 to 1.75
- b_outer: bfloat16 [4, 768], P('expert'), may hold values from -6 to 6
- image_count: int32 [32], P(('expert', 'hidden', 'dp')), may hold values from 1 to 3, as said below
- patches: int32 [32], P(('expert', 'hidden', 'dp')), may hold values from 196 to 576, as said below
- picks: int32 [20480, 2], P(('expert', 'hidden', 'dp')), may hold values from 0 to 3, as said below
- slots: int32 [20480, 2], P(('expert', 'hidden', 'dp')), may hold values from -1 to 335, as said below
Outputs:
- block_out: bfloat16 [20480, 768], P(('expert', 'hidden', 'dp'))
- grad_tokens: float32 [20480, 768], P(('expert', 'hidden', 'dp'))
- grad_ln1_gain: float32 [768], replicated
- grad_ln1_shift: float32 [768], replicated
- grad_w_query: float32 [768, 768], replicated
- grad_w_key: float32 [768, 768], replicated
- grad_w_value: float32 [768, 768], replicated
- grad_w_output: float32 [768, 768], replicated
- grad_ln2_gain: float32 [768], replicated
- grad_ln2_shift: float32 [768], replicated
- grad_w_router: float32 [768, 4], replicated
- grad_w_inner: float32 [4, 768, 3072], P('expert', None, 'hidden')
- grad_b_inner: float32 [4, 3072], P('expert', 'hidden')
- grad_w_outer: float32 [4, 3072, 768], P('expert', 'hidden')
- grad_b_outer: float32 [4, 768], P('expert')
Inputs may be any that keep to these rules, and one draw needn't show every extreme that they name: `image_count`: rows of a device are its images in order, each of patches rows, then padding. Each device's images are all of 196 or all of 576 patches; image_count times patches is at most 640. `picks`: the two experts of a row differ. `slots`: slot of the choice in the buffer of expert picks[t, k] for the rows of t's device, -1 where the choice is dropped and for both choices of a padding row; on one device no two choices share an expert and a slot.
All inputs are finite; a program needn't handle non-finite values.
Results may differ from a plain program's by a relative error of at most 0.017.
Values may be sent and summed in bfloat16 or wider, within the bound.
No kernel may reach another device: no remote copies, remote signals or barrier semaphores. Data moves between devices by JAX's collectives and lax.ppermute only.
A program may use at most 192 MiB of HBM per device.

v0:
```python
import jax
import jax.numpy as jnp
from jax import lax
from jax.sharding import PartitionSpec as P

HEADS = 12
QBLOCK = 640


NORM_EPS = 1e-06
MASKED = -1e30


def norm_rows(values, gain_vec, shift_vec):
    center = jnp.mean(values, axis=-1, keepdims=True)
    centered = values - center
    moment = jnp.mean(centered * centered, axis=-1, keepdims=True)
    return centered * lax.rsqrt(moment + NORM_EPS) * gain_vec + shift_vec


def smooth_gate(values):
    return jax.nn.gelu(values, approximate=True)


def router_softmax(logits):
    largest = jnp.max(logits, axis=-1, keepdims=True)
    powers = jnp.exp(logits - largest)
    return powers / jnp.sum(powers, axis=-1, keepdims=True)


def by_expert(received, groups, capacity):
    per_device = received.shape[0] // groups
    model_width = received.shape[-1]
    return (
        received.reshape(groups, per_device, capacity, model_width)
        .transpose(1, 0, 2, 3)
        .reshape(per_device, groups * capacity, model_width)
    )


def by_source(results, groups, capacity):
    per_device = results.shape[0]
    model_width = results.shape[-1]
    return (
        results.reshape(per_device, groups, capacity, model_width)
        .transpose(1, 0, 2, 3)
        .reshape(groups * per_device, capacity, model_width)
    )


def pack_rows(pair_rows, dest_index, experts, capacity):
    model_width = pair_rows.shape[-1]
    flattened = pair_rows.reshape(-1, model_width)
    buffer = jnp.zeros((experts * capacity, model_width), pair_rows.dtype)
    buffer = buffer.at[dest_index.reshape(-1)].set(flattened, mode="drop")
    return buffer.reshape(experts, capacity, model_width)


def unpack_rows(buffer, dest_index, assigned_float):
    model_width = buffer.shape[-1]
    flattened = buffer.reshape(-1, model_width)
    clipped = jnp.minimum(dest_index, flattened.shape[0] - 1)
    fetched = jnp.take(flattened, clipped.reshape(-1), axis=0).reshape(
        dest_index.shape + (model_width,)
    )
    return fetched.astype(jnp.float32) * assigned_float[:, :, None]


def shards(
    tokens,
    cotangent,
    ln1_gain,
    ln1_shift,
    w_query,
    w_key,
    w_value,
    w_output,
    ln2_gain,
    ln2_shift,
    w_router,
    w_inner,
    b_inner,
    w_outer,
    b_outer,
    image_count,
    patches,
    picks,
    slots,
):
    rows_dev, model_width = tokens.shape
    experts = w_router.shape[1]
    groups = lax.axis_size("expert")
    capacity = 21 * rows_dev // (10 * experts)
    head_dim = model_width // HEADS
    score_scale = head_dim ** (-0.5)
    block_rows = min(QBLOCK, rows_dev)
    blocks = rows_dev // block_rows
    position = jnp.arange(rows_dev, dtype=jnp.int32)
    patch_rows = patches[0]
    live_mask = position < image_count[0] * patch_rows
    segment = jnp.where(live_mask, position // patch_rows, -1 - position)
    live_rows = live_mask.astype(jnp.float32)[:, None]
    assigned = slots >= 0
    assigned_float = assigned.astype(jnp.float32)
    dest_index = jnp.where(assigned, picks * capacity + slots, experts * capacity)
    inputs = tokens.astype(jnp.float32)
    normed_one, norm_one_back = jax.vjp(norm_rows, inputs, ln1_gain, ln1_shift)
    normed_one = normed_one.astype(jnp.bfloat16)
    query = jnp.dot(normed_one, w_query, preferred_element_type=jnp.float32).astype(jnp.bfloat16)
    key_rows = jnp.dot(normed_one, w_key, preferred_element_type=jnp.float32).astype(jnp.bfloat16)
    value_rows = jnp.dot(normed_one, w_value, preferred_element_type=jnp.float32).astype(
        jnp.bfloat16
    )
    query_heads = query.reshape(rows_dev, HEADS, head_dim)
    key_heads = key_rows.reshape(rows_dev, HEADS, head_dim)
    value_heads = value_rows.reshape(rows_dev, HEADS, head_dim)

    def masked_scores():
        raw_scores = (
            jnp.einsum("thd,shd->hts", query_heads, key_heads, preferred_element_type=jnp.float32)
            * score_scale
        )
        allowed = segment[:, None] == segment[None, :]
        return (jnp.where(allowed[None], raw_scores, MASKED), query_heads)

    def attend_forward(offset):
        scores, unused = masked_scores()
        largest = jnp.max(scores, axis=-1, keepdims=True)
        powers = jnp.exp(scores - largest)
        denominator = jnp.sum(powers, axis=-1, keepdims=True)
        weights = (powers / denominator).astype(jnp.bfloat16)
        mixed_block = jnp.einsum(
            "hts,shd->thd", weights, value_heads, preferred_element_type=jnp.float32
        )
        return (mixed_block.astype(jnp.bfloat16), (largest + jnp.log(denominator))[:, :, 0])

    offsets = jnp.arange(blocks, dtype=jnp.int32) * block_rows
    mixed_blocks, log_totals = lax.map(attend_forward, offsets)
    mixed_rows = mixed_blocks.reshape(rows_dev, model_width)
    residual_one = inputs + jnp.dot(mixed_rows, w_output, preferred_element_type=jnp.float32)
    normed_two, norm_two_back = jax.vjp(norm_rows, residual_one, ln2_gain, ln2_shift)
    normed_two = normed_two.astype(jnp.bfloat16)
    logits = jnp.dot(normed_two, w_router, preferred_element_type=jnp.float32)
    gate_probs, gates_back = jax.vjp(router_softmax, logits)
    chosen = jnp.take_along_axis(gate_probs, picks, axis=1) * assigned_float
    pair_rows = jnp.broadcast_to(normed_two[:, None, :], (rows_dev, 2, model_width))
    outgoing = pack_rows(pair_rows, dest_index, experts, capacity)
    inbound = by_expert(
        lax.all_to_all(outgoing, "expert", split_axis=0, concat_axis=0, tiled=True),
        groups,
        capacity,
    )
    inner_all, inner_bias, outer_all = (
        lax.all_gather(w_inner, "hidden", axis=2, tiled=True),
        lax.all_gather(b_inner, "hidden", axis=1, tiled=True),
        lax.all_gather(w_outer, "hidden", axis=1, tiled=True),
    )
    inner_bias_f = inner_bias.astype(jnp.float32)[:, None, :]
    pre_act = (
        jnp.einsum("erd,edf->erf", inbound, inner_all, preferred_element_type=jnp.float32)
        + inner_bias_f
    )
    hidden_act = smooth_gate(pre_act).astype(jnp.bfloat16)
    outer_terms = jnp.einsum(
        "erf,efd->erd", hidden_act, outer_all, preferred_element_type=jnp.float32
    )
    expert_out = (outer_terms + b_outer.astype(jnp.float32)[:, None, :]).astype(jnp.bfloat16)
    returned = lax.all_to_all(
        by_source(expert_out, groups, capacity), "expert", split_axis=0, concat_axis=0, tiled=True
    )
    fetched = unpack_rows(returned, dest_index, assigned_float)
    mixture = jnp.sum(chosen[:, :, None] * fetched, axis=1)
    block_out = ((residual_one + mixture) * live_rows).astype(jnp.bfloat16)
    grad_out = cotangent.astype(jnp.float32) * live_rows
    grad_chosen = jnp.sum(grad_out[:, None, :] * fetched, axis=-1) * assigned_float
    expert_ids = jnp.arange(experts, dtype=jnp.int32)
    grad_gate = jnp.sum(
        (picks[:, :, None] == expert_ids[None, None, :]).astype(jnp.float32)
        * grad_chosen[:, :, None],
        axis=1,
    )
    grad_logits = gates_back(grad_gate)[0]
    grad_pair = (chosen[:, :, None] * grad_out[:, None, :]).astype(jnp.bfloat16)
    grad_inbound = by_expert(
        lax.all_to_all(
            pack_rows(grad_pair, dest_index, experts, capacity),
            "expert",
            split_axis=0,
            concat_axis=0,
            tiled=True,
        ),
        groups,
        capacity,
    )
    pre_again = (
        jnp.einsum("erd,edf->erf", inbound, inner_all, preferred_element_type=jnp.float32)
        + inner_bias_f
    )
    act_again, gate_back = jax.vjp(smooth_gate, pre_again)
    act_again = act_again.astype(jnp.bfloat16)
    grad_act = jnp.einsum(
        "erd,efd->erf", grad_inbound, outer_all, preferred_element_type=jnp.float32
    )
    grad_pre = gate_back(grad_act)[0].astype(jnp.bfloat16)
    grad_outer_w = jnp.einsum(
        "erf,erd->efd", act_again, grad_inbound, preferred_element_type=jnp.float32
    )
    grad_outer_b = jnp.sum(grad_inbound.astype(jnp.float32), axis=1)
    grad_inner_w = jnp.einsum("erd,erf->edf", inbound, grad_pre, preferred_element_type=jnp.float32)
    grad_inner_b = jnp.sum(grad_pre.astype(jnp.float32), axis=1)
    back_terms = jnp.einsum("erf,edf->erd", grad_pre, inner_all, preferred_element_type=jnp.float32)
    grad_inner_w, grad_inner_b, grad_outer_w = (
        lax.psum_scatter(
            grad_inner_w.astype(jnp.bfloat16), "hidden", scatter_dimension=2, tiled=True
        ).astype(jnp.float32),
        lax.psum_scatter(
            grad_inner_b.astype(jnp.bfloat16), "hidden", scatter_dimension=1, tiled=True
        ).astype(jnp.float32),
        lax.psum_scatter(
            grad_outer_w.astype(jnp.bfloat16), "hidden", scatter_dimension=1, tiled=True
        ).astype(jnp.float32),
    )
    grad_outer_b = lax.psum(grad_outer_b, "hidden")
    grad_returned = lax.all_to_all(
        by_source(back_terms.astype(jnp.bfloat16), groups, capacity),
        "expert",
        split_axis=0,
        concat_axis=0,
        tiled=True,
    )
    router_float = w_router.astype(jnp.float32)
    grad_normed_two = jnp.sum(unpack_rows(grad_returned, dest_index, assigned_float), axis=1)
    grad_normed_two = grad_normed_two + jnp.einsum(
        "te,de->td", grad_logits, router_float, precision=lax.Precision.HIGHEST
    )
    grad_router = jnp.einsum(
        "td,te->de", normed_two.astype(jnp.float32), grad_logits, precision=lax.Precision.HIGHEST
    )
    grad_norm_part, grad_gain_two, grad_shift_two = norm_two_back(grad_normed_two)
    grad_residual = grad_out + grad_norm_part
    grad_branch = grad_residual.astype(jnp.bfloat16)
    grad_w_output = jnp.einsum(
        "td,te->de", mixed_rows, grad_branch, preferred_element_type=jnp.float32
    )
    grad_mixed = jnp.einsum(
        "te,de->td", grad_branch, w_output, preferred_element_type=jnp.float32
    ).astype(jnp.bfloat16)

    def attend_backward(running, block_inputs):
        offset, grad_block, log_block = block_inputs
        scores, query_block = masked_scores()
        weights_full = jnp.exp(scores - log_block[:, :, None])
        grad_weights = jnp.einsum(
            "thd,shd->hts", grad_block, value_heads, preferred_element_type=jnp.float32
        )
        grad_value_acc = running[1] + jnp.einsum(
            "hts,thd->shd",
            weights_full.astype(jnp.bfloat16),
            grad_block,
            preferred_element_type=jnp.float32,
        )
        row_inner = jnp.sum(grad_weights * weights_full, axis=-1, keepdims=True)
        grad_scores = (weights_full * (grad_weights - row_inner)).astype(jnp.bfloat16)
        grad_query_block = (
            jnp.einsum("hts,shd->thd", grad_scores, key_heads, preferred_element_type=jnp.float32)
            * score_scale
        )
        grad_key_acc = (
            running[0]
            + jnp.einsum(
                "hts,thd->shd", grad_scores, query_block, preferred_element_type=jnp.float32
            )
            * score_scale
        )
        return ((grad_key_acc, grad_value_acc), grad_query_block)

    zero_heads = jnp.zeros((rows_dev, HEADS, head_dim), jnp.float32)
    grad_mixed_blocks = grad_mixed.reshape(blocks, block_rows, HEADS, head_dim)
    (grad_key_heads, grad_value_heads), grad_query_blocks = lax.scan(
        attend_backward, (zero_heads, zero_heads), (offsets, grad_mixed_blocks, log_totals)
    )
    grad_query = grad_query_blocks.reshape(rows_dev, model_width).astype(jnp.bfloat16)
    grad_key = grad_key_heads.reshape(rows_dev, model_width).astype(jnp.bfloat16)
    grad_value = grad_value_heads.reshape(rows_dev, model_width).astype(jnp.bfloat16)
    grad_w_query = jnp.einsum(
        "td,te->de", normed_one, grad_query, preferred_element_type=jnp.float32
    )
    grad_w_key = jnp.einsum("td,te->de", normed_one, grad_key, preferred_element_type=jnp.float32)
    grad_w_value = jnp.einsum(
        "td,te->de", normed_one, grad_value, preferred_element_type=jnp.float32
    )
    grad_normed_one = jnp.einsum(
        "te,de->td", grad_query, w_query, preferred_element_type=jnp.float32
    )
    grad_normed_one = grad_normed_one + jnp.einsum(
        "te,de->td", grad_key, w_key, preferred_element_type=jnp.float32
    )
    grad_normed_one = grad_normed_one + jnp.einsum(
        "te,de->td", grad_value, w_value, preferred_element_type=jnp.float32
    )
    grad_input_part, grad_gain_one, grad_shift_one = norm_one_back(grad_normed_one)
    grad_tokens = grad_residual + grad_input_part
    expert_sums_grad = (
        lax.psum(grad_inner_w.astype(jnp.bfloat16), "dp").astype(jnp.float32),
        lax.psum(grad_inner_b.astype(jnp.bfloat16), "dp").astype(jnp.float32),
        lax.psum(grad_outer_w.astype(jnp.bfloat16), "dp").astype(jnp.float32),
        lax.psum(grad_outer_b.astype(jnp.bfloat16), "dp").astype(jnp.float32),
    )
    shared = lax.psum(
        (
            grad_w_query,
            grad_w_key,
            grad_w_value,
            grad_w_output,
            grad_router,
            grad_gain_one,
            grad_shift_one,
            grad_gain_two,
            grad_shift_two,
        ),
        ("expert", "hidden", "dp"),
    )
    return (
        block_out,
        grad_tokens,
        shared[5],
        shared[6],
        shared[0],
        shared[1],
        shared[2],
        shared[3],
        shared[7],
        shared[8],
        shared[4],
        expert_sums_grad[0],
        expert_sums_grad[1],
        expert_sums_grad[2],
        expert_sums_grad[3],
    )


def solution(mesh):
    placed = (
        P(("expert", "hidden", "dp"), None),
        P(("expert", "hidden", "dp"), None),
        P(),
        P(),
        P(),
        P(),
        P(),
        P(),
        P(),
        P(),
        P(),
        P("expert", None, "hidden"),
        P("expert", "hidden"),
        P("expert", "hidden", None),
        P("expert", None),
        P(("expert", "hidden", "dp")),
        P(("expert", "hidden", "dp")),
        P(("expert", "hidden", "dp"), None),
        P(("expert", "hidden", "dp"), None),
    )
    return jax.shard_map(
        shards,
        mesh=mesh,
        in_specs=placed,
        out_specs=(
            P(("expert", "hidden", "dp"), None),
            P(("expert", "hidden", "dp"), None),
            P(),
            P(),
            P(),
            P(),
            P(),
            P(),
            P(),
            P(),
            P(),
            P("expert", None, "hidden"),
            P("expert", "hidden"),
            P("expert", "hidden", None),
            P("expert", None),
        ),
        check_vma=False,
    )
```

profile of v0, /device:TPU:0, one launch (start us, length us, event | category | flops | bytes accessed | tf_op | source)
XLA Modules:
  0.0 788.2 jit_solution(1417398133769751573)
XLA Ops:
  25.4 11.6 %fusion.82 = (f32[12,640]{1,0:T(8,128)}, f32[12,640,640]{1,2,0:T(8,128)}) fusion(bf16[640,12,64]{0,2,1:T(8,128)(2,1)} %bitcast.104, bf16[640,12,64]{0,2,1:T(8,128)(2,1)S(1)} %bitcast.102, pred[640,640]{0,1:T(8,128)(4,1)S(1)} %broadcast_compare_fusion), kind=kOutput, calls=%fused_computation.150 | convolution fusion | flops 643883520 | bytes 22067200 | tf_op jit(solution)/shard_map/while/body/eval_jaxpr/thd,shd->hts/dot_general | solution.py:120
  37.0 9.3 %fusion = f32[12,640]{1,0:T(8,128)S(1)} fusion(f32[12,640,640]{1,2,0:T(8,128)} %get-tuple-element.103, f32[12,640]{1,0:T(8,128)} %get-tuple-element.102), kind=kLoop, calls=%fused_computation.13 | loop fusion | flops 9822720 | bytes 19722240 | tf_op jit(solution)/shard_map/while/body/eval_jaxpr/reduce_sum | solution.py:130
  46.4 8.8 %fusion.43 = bf16[12,64,640]{2,1,0:T(8,128)(2,1)S(1)} fusion(bf16[640,12,64]{0,2,1:T(8,128)(2,1)S(1)} %bitcast.111, f32[12,640,640]{1,2,0:T(8,128)} %get-tuple-element.103, f32[12,640]{1,0:T(8,128)S(1)} %fusion, f32[12,640]{1,0:T(8,128)S(1)} %copy-done.35), kind=kOutput, calls=%fused_computation.77 | convolution fusion | flops 644382720 | bytes 21688320 | tf_op jit(solution)/shard_map/while/body/eval_jaxpr/hts,shd->thd/dot_general | solution.py:132
  62.7 10.2 %scatter_custom_fusion = bf16[1344,768]{1,0:T(8,128)(2,1)} fusion(s32[1280]{0:T(1024)S(1)} %fusion.54, bf16[1280,768]{1,0:T(8,128)(2,1)} %reshape.421, bf16[]{:T(256)} %constant.84.clone.1), kind=kCustom, calls=%fused_computation.84 | custom fusion | bytes 2064896 | tf_op jit(solution)/shard_map/scatter | solution.py:55
  72.9 6.2 all-to-all-start
  81.7 44.8 %all-to-all-done = bf16[4,336,768]{2,1,0:T(8,128)(2,1)S(1)} async-done(((bf16[4,336,768]{2,1,0:T(8,128)(2,1)}), bf16[4,336,768]{2,1,0:T(8,128)(2,1)S(1)}, u32[]{:S(2)}, u32[]{:S(2)}) %all-to-all-start) | async-done | bytes 2064416 | tf_op jit(solution)/shard_map/all_to_all | solution.py:149
  126.5 17.0 %multiply_convert_fusion.1 = (bf16[1344,3072]{1,0:T(8,128)(2,1)}, f32[1344,3072]{1,0:T(8,128)}) fusion(f32[3072]{0:T(1024)S(1)} %bitcast.124, bf16[1344,768]{1,0:T(8,128)(2,1)S(1)} %bitcast.115, bf16[1,768,3072]{2,1,0:T(8,128)(2,1)} %all-gather.3.cloned.1.call-done), kind=kOutput, calls=%fused_computation.21 | convolution fusion | flops 6383075328 | bytes 31567872 | tf_op jit(solution)/shard_map/erd,edf->erf/dot_general | solution.py:160
  143.6 11.3 %add_convert_fusion = bf16[1344,768]{1,0:T(8,128)(2,1)} fusion(bf16[1344,3072]{1,0:T(8,128)(2,1)} %get-tuple-element.106, bf16[1,3072,768]{2,1,0:T(8,128)(2,1)} %all-gather.5.cloned.1.call-done, f32[768]{0:T(1024)S(1)} %convert_reduce_fusion.3), kind=kOutput, calls=%fused_computation.39 | convolution fusion | flops 6343852032 | bytes 15043584 | tf_op jit(solution)/shard_map/erf,efd->erd/dot_general | solution.py:164
  177.4 28.0 %all-to-all-done.1 = bf16[4,336,768]{2,1,0:T(8,128)(2,1)S(1)} async-done(((bf16[4,336,768]{2,1,0:T(8,128)(2,1)}), bf16[4,336,768]{2,1,0:T(8,128)(2,1)S(1)}, u32[]{:S(2)}, u32[]{:S(2)}) %all-to-all-start.1) | async-done | bytes 2064416 | tf_op jit(solution)/shard_map/all_to_all | solution.py:168
  216.5 11.0 %gather_fusion = f32[1280]{0:T(1024)S(1)} fusion(f32[640,4]{0,1:T(4,128)S(1)} %get-tuple-element.98, s32[1280]{0:T(1024)S(1)} %reshape.411), kind=kCustom, calls=%fused_computation.2 | custom fusion | bytes 20480 | tf_op jit(solution)/shard_map/jit(take_along_axis)/gather | solution.py:145
  229.0 14.1 %scatter_custom_fusion.1 = bf16[1344,768]{1,0:T(8,128)(2,1)S(1)} fusion(s32[1280]{0:T(1024)S(1)} %fusion.54, f32[1280,768]{1,0:T(8,128)} %mul.336, f32[1280]{0:T(1024)S(1)} %mul.333, bf16[]{:T(256)} %constant.84.clone.1), kind=kCustom, calls=%fused_computation.61 | custom fusion | flops 1966080 | bytes 6004738 | tf_op jit(solution)/shard_map/scatter | solution.py:55
  243.1 49.7 %all_to_all.20 = bf16[4,336,768]{2,1,0:T(8,128)(2,1)S(1)} all-to-all(bf16[4,336,768]{2,1,0:T(8,128)(2,1)S(1)} %bitcast.108), channel_id=1, replica_groups=mesh['expert'=4,'hidden'=2,'dp'=4] {'expert'}, dimensions={0} | all-to-all | bytes 4128768 | tf_op jit(solution)/shard_map/all_to_all | solution.py:185
  294.1 12.7 %fusion.24 = bf16[1,3072,768]{2,1,0:T(8,128)(2,1)} fusion(bf16[1344,3072]{1,0:T(8,128)(2,1)} %get-tuple-element.106, bf16[1344,768]{1,0:T(8,128)(2,1)S(1)} %bitcast.109), kind=kOutput, calls=%fused_computation.37 | convolution fusion | flops 6344146944 | bytes 15040512 | tf_op jit(solution)/shard_map/erf,erd->efd/dot_general | solution.py:205
  308.4 19.5 %fusion.85 = (bf16[3072]{0:T(1024)(128)(2,1)S(1)}, bf16[1344,3072]{1,0:T(8,128)(2,1)S(1)}) fusion(f32[1344,3072]{1,0:T(8,128)} %get-tuple-element.107, f32[3072]{0:T(1024)S(1)} %bitcast.125, bf16[1344,768]{1,0:T(8,128)(2,1)S(1)} %bitcast.110, bf16[1,3072,768]{2,1,0:T(8,128)(2,1)} %all-gather.5.cloned.1.call-done), kind=kOutput, calls=%fused_computation.153 | convolution fusion | flops 6432617472 | bytes 31574016 | tf_op jit(solution)/shard_map/erd,efd->erf/dot_general | solution.py:201
  331.3 9.1 %fusion.23 = bf16[1,768,3072]{2,1,0:T(8,128)(2,1)} fusion(bf16[1344,768]{1,0:T(8,128)(2,1)S(1)} %bitcast.116, bf16[1344,3072]{1,0:T(8,128)(2,1)S(1)} %get-tuple-element.115), kind=kOutput, calls=%fused_computation.36 | convolution fusion | flops 6344146944 | bytes 15040512 | tf_op jit(solution)/shard_map/erd,erf->edf/dot_general | solution.py:209
  340.4 11.4 %fusion.27 = bf16[1344,768]{1,0:T(8,128)(2,1)} fusion(bf16[1344,3072]{1,0:T(8,128)(2,1)} %copy-done.79, bf16[1,768,3072]{2,1,0:T(8,128)(2,1)} %all-gather.3.cloned.1.call-done), kind=kOutput, calls=%fused_computation.44 | convolution fusion | flops 6342819840 | bytes 15040512 | tf_op jit(solution)/shard_map/erf,edf->erd/dot_general | solution.py:211
  357.2 45.1 %all-to-all-done.3 = bf16[4,336,768]{2,1,0:T(8,128)(2,1)S(1)} async-done(((bf16[4,336,768]{2,1,0:T(8,128)(2,1)}), bf16[4,336,768]{2,1,0:T(8,128)(2,1)S(1)}, u32[]{:S(2)}, u32[]{:S(2)}) %all-to-all-start.3) | async-done | bytes 2064416 | tf_op jit(solution)/shard_map/all_to_all | solution.py:224
  424.8 11.9 %multiply_reduce_fusion.2 = (f32[640,768]{1,0:T(8,128)S(1)}, f32[640,768]{1,0:T(8,128)S(1)}) fusion(f32[640,2,768]{2,1,0:T(2,128)} %reshape.394, f32[640,2]{1,0:T(8,128)S(1)} %copy-done.22, f32[640,2,768]{2,1,0:T(2,128)} %reshape.393, f32[640,2]{1,0:T(8,128)S(1)} %copy-done.24), kind=kLoop, calls=%fused_computation.41 | loop fusion | flops 3932160 | bytes 11806720 | tf_op jit(solution)/shard_map/reduce_sum | solution.py:232
  445.7 12.3 %multiply_reduce_fusion = (f32[12,640]{1,0:T(8,128)S(1)}, f32[12,640,640]{1,2,0:T(8,128)}) fusion(f32[12,640,640]{1,2,0:T(8,128)} %get-tuple-element.103, f32[12,640]{1,0:T(8,128)S(1)} %log_add_fusion, bf16[640,12,64]{0,2,1:T(8,128)(2,1)S(1)} %bitcast.106, bf16[640,12,64]{0,2,1:T(8,128)(2,1)S(1)} %bitcast.112), kind=kOutput, calls=%fused_computation.8 | convolution fusion | flops 643883520 | bytes 41349120 | tf_op jit(solution)/shard_map/while/body/eval_jaxpr/thd,shd->hts/dot_general | solution.py:253
  458.1 14.8 %multiply_convert_fusion = bf16[12,640,640]{1,2,0:T(8,128)(2,1)S(1)} fusion(f32[12,640,640]{1,2,0:T(8,128)} %get-tuple-element.112, f32[12,640,640]{1,2,0:T(8,128)} %get-tuple-element.103, f32[12,640]{1,0:T(8,128)S(1)} %get-tuple-element.111, f32[12,640]{1,0:T(8,128)S(1)} %log_add_fusion), kind=kLoop, calls=%fused_computation.7 | loop fusion | flops 19660800 | bytes 49213440 | tf_op jit(solution)/shard_map/while/body/eval_jaxpr/convert_element_type | solution.py:263
  485.6 10.1 %fusion.44 = bf16[12,64,640]{2,1,0:T(8,128)(2,1)S(1)} fusion(bf16[640,12,64]{0,2,1:T(8,128)(2,1)S(1)} %bitcast.107, f32[12,640,640]{1,2,0:T(8,128)} %get-tuple-element.103, f32[12,640]{1,0:T(8,128)S(1)} %log_add_fusion), kind=kOutput, calls=%fused_computation.78 | convolution fusion | flops 639467520 | bytes 21657600 | tf_op jit(solution)/shard_map/while/body/eval_jaxpr/hts,thd->shd/dot_general | solution.py:256
  510.5 10.4 %all-reduce.2 = (bf16[1,1536]{1,0:T(2,128)(2,1)S(1)}, bf16[1,768]{1,0:T(2,128)(2,1)S(1)}) all-reduce(bf16[1,1536]{1,0:T(2,128)(2,1)S(1)} %copy.126, bf16[1,768]{1,0:T(2,128)(2,1)S(1)} %psum.110), channel_id=1, replica_groups=mesh['expert'=4,'hidden'=2,'dp'=4] {'dp'}, use_global_device_ids=true, to_apply=%region_39.41 | all-reduce | flops 2304 | bytes 9216 | tf_op jit(solution)/shard_map/psum | solution.py:305
  529.5 38.0 %all-reduce = (f32[768]{0:T(1024)}, f32[768]{0:T(1024)}, f32[768]{0:T(1024)}, f32[768]{0:T(1024)}, f32[768,4]{0,1:T(4,128)}) all-reduce(f32[768]{0:T(1024)S(1)} %get-tuple-element.69, f32[768]{0:T(1024)S(1)} %get-tuple-element.72, ...), channel_id=1, replica_groups=mesh['expert'=4,'hidden'=2,'dp'=4] {'expert','hidden','dp'}, use_global_device_ids=true, to_apply=%region_23.25 | all-reduce | flops 6144 | bytes 49152 | tf_op jit(solution)/shard_map/psum | solution.py:309
  578.6 192.7 %all-reduce.7.cloned.1.call-done = (f32[768,768]{1,0:T(8,128)}, f32[768,768]{1,0:T(8,128)}, f32[768,768]{1,0:T(8,128)}, f32[768,768]{1,0:T(8,128)}) async-done(((f32[768,768]{1,0:T(8,128)}, f32[768,768]{1,0:T(8,128)}, f32[768,768]{1,0:T(8,128)}, f32[768,768]{1,0:T(8,128)}), (f32[768,768]{1,0:T(8,128)}, f32[768,768]{1,0:T(8,128)}, f32[768,768]{1,0:T(8,128)}, ...) | async-done | bytes 9437200 | tf_op jit(solution)/shard_map/psum | solution.py:309
  (279 shorter events, 161.5 us)
Async XLA Ops:
  7.2 12.9 %copy-start = (bf16[768,768]{1,0:T(8,128)(2,1)S(1)}, bf16[768,768]{1,0:T(8,128)(2,1)}, u32[]{:S(2)}) copy-start(bf16[768,768]{1,0:T(8,128)(2,1)} %param.27) | copy-start | bytes 3538948
  7.2 119.3 %all-gather.3.cloned.1.call-start = ((), (), s32[]{:S(2)}) async-start(), calls=%async_computation.7 | async-start | bytes 7077888 | tf_op jit(solution)/shard_map/all_gather | solution.py:154
  72.9 53.6 %all-to-all-start = ((bf16[4,336,768]{2,1,0:T(8,128)(2,1)}), bf16[4,336,768]{2,1,0:T(8,128)(2,1)S(1)}, u32[]{:S(2)}, u32[]{:S(2)}) async-start(bf16[4,336,768]{2,1,0:T(8,128)(2,1)} %bitcast.8), calls=%async_computation | async-start | bytes 4128768 | tf_op jit(solution)/shard_map/all_to_all | solution.py:149
  79.1 64.5 %all-gather.5.cloned.1.call-start = ((), (), s32[]{:S(2)}) async-start(), calls=%async_computation.8 | async-start | bytes 7077888 | tf_op jit(solution)/shard_map/all_gather | solution.py:156
  126.5 17.0 %copy-start.29 = (bf16[4,336,768]{2,1,0:T(8,128)(2,1)}, bf16[4,336,768]{2,1,0:T(8,128)(2,1)S(1)}, u32[]{:S(2)}) copy-start(bf16[4,336,768]{2,1,0:T(8,128)(2,1)S(1)} %all-to-all-done) | copy-start | bytes 6193156
  154.8 50.6 %all-to-all-start.1 = ((bf16[4,336,768]{2,1,0:T(8,128)(2,1)}), bf16[4,336,768]{2,1,0:T(8,128)(2,1)S(1)}, u32[]{:S(2)}, u32[]{:S(2)}) async-start(bf16[4,336,768]{2,1,0:T(8,128)(2,1)} %bitcast.117), calls=%async_computation.1 | async-start | bytes 4128768 | tf_op jit(solution)/shard_map/all_to_all | solution.py:168
  158.5 299.6 %reduce-scatter.8.cloned.1.call-start = ((), (), s32[]{:S(2)}) async-start(), calls=%async_computation.10 | async-start | bytes 7077888 | tf_op jit(solution)/shard_map/reduce_scatter | solution.py:219
  175.7 34.6 %copy-start.46 = (s32[2048]{0:T(1024)}, s32[2048]{0:T(1024)S(1)}, u32[]{:S(2)}) copy-start(s32[2048]{0:T(1024)S(1)} %pad_clamp_fusion) | copy-start | bytes 24580
  177.4 32.9 %copy-start.65 = (pred[1280]{0:T(1024)(128)(4,1)}, pred[1280]{0:T(1024)(128)(4,1)S(1)}, u32[]{:S(2)}) copy-start(pred[1280]{0:T(1024)(128)(4,1)S(1)} %compare_and_fusion) | copy-start | bytes 3844
  306.8 151.2 %reduce-scatter.6.cloned.1.call-start = ((), (), s32[]{:S(2)}) async-start(), calls=%async_computation.9 | async-start | bytes 7077888 | tf_op jit(solution)/shard_map/reduce_scatter | solution.py:213
  308.4 22.9 %copy-start.30 = (bf16[4,336,768]{2,1,0:T(8,128)(2,1)S(1)}, bf16[4,336,768]{2,1,0:T(8,128)(2,1)}, u32[]{:S(2)}) copy-start(bf16[4,336,768]{2,1,0:T(8,128)(2,1)} %copy-done.29) | copy-start | bytes 6193156
  351.8 50.5 %copy-start.47 = (s32[2048]{0:T(1024)S(1)}, s32[2048]{0:T(1024)}, u32[]{:S(2)}) copy-start(s32[2048]{0:T(1024)} %copy-done.46) | copy-start | bytes 24580
  351.9 50.5 %all-to-all-start.3 = ((bf16[4,336,768]{2,1,0:T(8,128)(2,1)}), bf16[4,336,768]{2,1,0:T(8,128)(2,1)S(1)}, u32[]{:S(2)}, u32[]{:S(2)}) async-start(bf16[4,336,768]{2,1,0:T(8,128)(2,1)} %bitcast.118), calls=%async_computation.3 | async-start | bytes 4128768 | tf_op jit(solution)/shard_map/all_to_all | solution.py:224
  355.6 153.7 %reduce-scatter.10.cloned.1.call-start = ((), (), s32[]{:S(2)}) async-start(), calls=%async_computation.11 | async-start | bytes 1179648
  357.2 214.3 %all-reduce.9.cloned.1.call-start = ((), (), s32[]{:S(2)}) async-start(), calls=%async_computation.13 | async-start | bytes 9437184 | tf_op jit(solution)/shard_map/psum | solution.py:304
  424.7 12.0 %copy-start.2 = (f32[640,768]{1,0:T(8,128)S(1)}, f32[640,768]{1,0:T(8,128)}, u32[]{:S(2)}) copy-start(f32[640,768]{1,0:T(8,128)} %copy-done.1) | copy-start | bytes 5898244
  424.7 12.0 %copy-start.40 = (f32[640]{0:T(1024)S(1)}, f32[640]{0:T(1024)}, u32[]{:S(2)}) copy-start(f32[640]{0:T(1024)} %copy-done.39) | copy-start | bytes 7684
  424.7 12.0 %copy-start.43 = (f32[640,4]{0,1:T(4,128)S(1)}, f32[640,4]{0,1:T(4,128)}, u32[]{:S(2)}) copy-start(f32[640,4]{0,1:T(4,128)} %get-tuple-element.92) | copy-start | bytes 30724
  424.7 12.0 %copy-start.51 = (f32[640]{0:T(1024)S(1)}, f32[640]{0:T(1024)}, u32[]{:S(2)}) copy-start(f32[640]{0:T(1024)} %copy-done.50) | copy-start | bytes 7684
  424.7 12.0 %copy-start.53 = (f32[768]{0:T(1024)S(1)}, f32[768]{0:T(1024)}, u32[]{:S(2)}) copy-start(f32[768]{0:T(1024)} %param.29) | copy-start | bytes 9220
  458.1 313.2 %all-reduce.7.cloned.1.call-start = ((), (), s32[]{:S(2)}) async-start(), calls=%async_computation.12 | async-start | bytes 18874368 | tf_op jit(solution)/shard_map/psum | solution.py:309
  458.1 14.8 %copy-start.10 = (bf16[640,768]{0,1:T(8,128)(2,1)S(1)}, bf16[640,768]{0,1:T(8,128)(2,1)}, u32[]{:S(2)}) copy-start(bf16[640,768]{0,1:T(8,128)(2,1)} %copy.105) | copy-start | bytes 2949124
  503.9 18.1 %copy-start.34 = (bf16[12,64,640]{2,1,0:T(8,128)(2,1)S(1)}, bf16[12,64,640]{2,1,0:T(8,128)(2,1)}, u32[]{:S(2)}) copy-start(bf16[12,64,640]{2,1,0:T(8,128)(2,1)} %copy-done.33) | copy-start | bytes 2949124
  527.2 40.3 %copy-start.17 = (bf16[640,768]{1,0:T(8,128)(2,1)S(1)}, bf16[640,768]{1,0:T(8,128)(2,1)}, u32[]{:S(2)}) copy-start(bf16[640,768]{1,0:T(8,128)(2,1)} %param.22) | copy-start | bytes 2949124
  (66 other events, 228.8 us)
Sparse Core Ops, SparseCore 0:
  9.6 17.1 all-gather.2
  81.5 15.9 all-gather.4
  307.0 11.6 reduce-scatter.7
  340.6 11.6 reduce-scatter.5
  358.4 9.6 reduce-scatter.9
  458.2 113.1 all-reduce.8
  579.3 191.9 all-reduce.6
where the time goes:
time: 798 us; the launch traced here: 788 us
  waiting for transfers between devices  312 us (39%)
  matrix products  161 us (20%)
  blocking collectives  103 us (13%)
  local copies, waits for them, and re-layouts  99.3 us (12%)
  other arithmetic  82.1 us (10%)
  between operations  16.7 us (2%)
  starting transfers between devices  13.8 us (2%)
    psum x1, waiting for transfers between devices, shards(): lax.psum((grad_w_query, grad_w_key, grad_w_value, grad_w_output, grad_rou...  193 us
    all_to_all x1, blocking collectives, shards(): lax.all_to_all(pack_rows(grad_pair, dest_index, experts, capacity), 'expe...  49.7 us
    all_to_all x1, waiting for transfers between devices, shards(): lax.all_to_all(by_source(back_terms.astype(jnp.bfloat16), groups, capacit...  45.1 us
    all_to_all x1, waiting for transfers between devices, shards(): lax.all_to_all(outgoing, 'expert', split_axis=0, concat_axis=0, tiled=True)  44.8 us
    psum x1, blocking collectives, shards(): lax.psum((grad_w_query, grad_w_key, grad_w_value, grad_w_output, grad_rou...  38 us
    unnamed x166, local copies, waits for them, and re-layouts  29.8 us
    all_to_all x1, waiting for transfers between devices, shards(): lax.all_to_all(by_source(expert_out, groups, capacity), 'expert', split_a...  28 us
    dot_general x1, matrix products, shards(): jnp.einsum('erd,efd->erf', grad_inbound, outer_all, preferred_element_typ...  19.5 us
  transfers between devices with their start and end apart: 10, of which 5 were waited for; matrix products, arithmetic and copies ran while one was open for 32% of the time, Pallas kernels for 0%

commit v1 on v0

v1 whole, which is shorter than its diff:
```python
import functools

import jax
import jax.numpy as jnp
from jax import lax
from jax.experimental import pallas as pl
from jax.experimental.pallas import tpu as pltpu
from jax.sharding import PartitionSpec as P

HEADS = 12
NORM_EPS = 1e-06
MASKED = -1e30
IMAGES_MAX = 8
BF = jnp.bfloat16
F32 = jnp.float32
VMEM_LIMIT = 56 * 1024 * 1024

VM = pltpu.VMEM
SMEM = pltpu.SMEM


def mm(a, b):
    return lax.dot_general(a, b, (((1,), (0,)), ((), ())), preferred_element_type=F32)


def mm_nt(a, b):
    return lax.dot_general(a, b, (((1,), (1,)), ((), ())), preferred_element_type=F32)


def mm_tn(a, b):
    return lax.dot_general(a, b, (((0,), (0,)), ((), ())), preferred_element_type=F32)


def standardize(values):
    center = jnp.mean(values, axis=-1, keepdims=True)
    centered = values - center
    moment = jnp.mean(centered * centered, axis=-1, keepdims=True)
    inv = lax.rsqrt(moment + NORM_EPS)
    return centered * inv, inv


def norm_back(grad_normed, gain, unit, inv):
    g = grad_normed * gain
    first = jnp.mean(g, axis=-1, keepdims=True)
    second = jnp.mean(g * unit, axis=-1, keepdims=True)
    return (g - first - unit * second) * inv


def targets(picks, slots, capacity):
    return jnp.where(slots >= 0, picks * capacity + slots, -1)


def pack_into(out_ref, rows_ref, pick_ref, slot_ref, capacity, step):
    dest = targets(pick_ref[...], slot_ref[...], capacity)
    total, rows = out_ref.shape[0], rows_ref.shape[0]
    for start in range(0, total, step):
        index = lax.broadcasted_iota(jnp.int32, (step, rows), 0) + start
        hit = (index == dest[0:1, :]) | (index == dest[1:2, :])
        out_ref[start : start + step, :] = mm(hit.astype(BF), rows_ref[...]).astype(BF)


def unpack_rows(buffer_ref, pick, slot, capacity):
    dest = targets(pick, slot, capacity)
    rows, total = dest.shape[0], buffer_ref.shape[0]
    index = lax.broadcasted_iota(jnp.int32, (rows, total), 1)
    hit = (index == dest[:, 0:1]) | (index == dest[:, 1:2])
    return mm(hit.astype(BF), buffer_ref[...])


def pack_step(total):
    for step in (448, 336, 224, 192, 112, 96, 64, 48, 32, 16):
        if total % step == 0:
            return step
    return total


def pack_kernel(pick_ref, slot_ref, rows_ref, out_ref, *, capacity):
    pack_into(out_ref, rows_ref, pick_ref, slot_ref, capacity, pack_step(out_ref.shape[0]))


def params():
    return pltpu.CompilerParams(vmem_limit_bytes=VMEM_LIMIT)


def whole(shape):
    return pl.BlockSpec(shape, lambda *_: (0,) * len(shape))


def pack(pick_rows, slot_rows, rows, total, capacity):
    count, width = rows.shape
    return pl.pallas_call(
        functools.partial(pack_kernel, capacity=capacity),
        out_shape=jax.ShapeDtypeStruct((total, width), BF),
        in_specs=[pl.BlockSpec(memory_space=VM)] * 3,
        out_specs=pl.BlockSpec(memory_space=VM),
        compiler_params=params(),
        cost_estimate=pl.CostEstimate(
            flops=2 * total * count * width, bytes_accessed=4 * total * width, transcendentals=0
        ),
        name="pack_rows",
    )(pick_rows, slot_rows, rows)


def classes(count, patch, rows, padding):
    row = lax.broadcasted_iota(jnp.int32, (rows, 1), 0)
    image = jnp.zeros((rows, 1), jnp.int32)
    for i in range(1, IMAGES_MAX):
        image = image + (row >= i * patch).astype(jnp.int32)
    return jnp.where(row < count * patch, image, padding)


def front_kernel(
    count_ref,
    patch_ref,
    tokens_ref,
    gain1_ref,
    shift1_ref,
    wq_ref,
    wk_ref,
    wv_ref,
    wo_ref,
    gain2_ref,
    shift2_ref,
    pick_ref,
    slot_ref,
    n1_ref,
    q_ref,
    k_ref,
    v_ref,
    p_ref,
    linv_ref,
    mixed_ref,
    res_ref,
    out_ref,
    n2_ref,
    *,
    capacity,
    head_dim,
    qb,
):
    j = pl.program_id(0)
    rows, width = tokens_ref.shape
    cols = wq_ref.shape[1]

    @pl.when(j == 0)
    def _():
        x = tokens_ref[...].astype(F32)
        unit, _ = standardize(x)
        n1_ref[...] = (unit * gain1_ref[...] + shift1_ref[...]).astype(BF)
        res_ref[...] = x

    n1 = n1_ref[...]
    q_ref[...] = mm(n1, wq_ref[...]).astype(BF)
    k_ref[...] = mm(n1, wk_ref[...]).astype(BF)
    v_ref[...] = mm(n1, wv_ref[...]).astype(BF)
    cls = classes(count_ref[0], patch_ref[0], rows, head_dim - 1)
    lane = lax.broadcasted_iota(jnp.int32, (rows, 2 * head_dim), 1)
    inner = lane % head_dim
    apart = jnp.where(inner == cls, 0.0, MASKED).astype(BF)
    member = jnp.where(inner == cls, 1.0, 0.0).astype(BF)
    ones = jnp.ones((rows, 2 * head_dim), BF)
    scale = head_dim ** (-0.5)
    for pair in range(cols // (2 * head_dim)):
        sl = slice(pair * 2 * head_dim, (pair + 1) * 2 * head_dim)
        q_pair = q_ref[:, sl] * jnp.asarray(scale, BF)
        k_pair = k_ref[:, sl]
        v_ext = jnp.concatenate([v_ref[:, sl], ones], axis=1)
        for h in range(2):
            mine = (lane >= h * head_dim) & (lane < (h + 1) * head_dim)
            qm = jnp.where(mine, q_pair, apart)
            km = jnp.where(mine, k_pair, member)
            for b in range(0, rows, qb):
                s = mm_nt(qm[b : b + qb], km)
                top = jnp.max(s, axis=-1, keepdims=True)
                p = jnp.exp(s - top).astype(BF)
                p_ref[pair * 2 + h, b : b + qb, :] = p
                ov = mm(p, v_ext)
                linv = 1.0 / ov[:, 2 * head_dim :]
                o = (ov[:, : 2 * head_dim] * linv).astype(BF)
                if h == 0:
                    mixed_ref[b : b + qb, sl] = o
                    linv_ref[b : b + qb, sl] = linv
                else:
                    keep = mine[b : b + qb]
                    mixed_ref[b : b + qb, sl] = jnp.where(keep, o, mixed_ref[b : b + qb, sl])
                    linv_ref[b : b + qb, sl] = jnp.where(keep, linv, linv_ref[b : b + qb, sl])
    res_ref[...] += mm(mixed_ref[...], wo_ref[...])

    @pl.when(j == pl.num_programs(0) - 1)
    def _():
        unit, _ = standardize(res_ref[...])
        n2_ref[...] = (unit * gain2_ref[...] + shift2_ref[...]).astype(BF)
        pack_into(out_ref, n2_ref, pick_ref, slot_ref, capacity, pack_step(out_ref.shape[0]))


def front(count, patch, tokens, g1, s1, wq, wk, wv, wo, g2, s2, pick_rows, slot_rows, total, capacity):
    rows, width = tokens.shape
    head_dim = width // HEADS
    quad = 4 * head_dim
    steps = width // quad
    col = pl.BlockSpec((width, quad), lambda j: (0, j))
    seq = pl.BlockSpec((rows, quad), lambda j: (0, j))
    smem = pl.BlockSpec(memory_space=SMEM)
    flops = 2 * rows * width * (4 * width + 2 * rows + total)
    return pl.pallas_call(
        functools.partial(front_kernel, capacity=capacity, head_dim=head_dim, qb=rows // 5),
        grid=(steps,),
        out_shape=(
            jax.ShapeDtypeStruct((rows, width), BF),
            jax.ShapeDtypeStruct((rows, width), BF),
            jax.ShapeDtypeStruct((rows, width), BF),
            jax.ShapeDtypeStruct((rows, width), BF),
            jax.ShapeDtypeStruct((HEADS, rows, rows), BF),
            jax.ShapeDtypeStruct((rows, width), F32),
            jax.ShapeDtypeStruct((rows, width), BF),
            jax.ShapeDtypeStruct((rows, width), F32),
            jax.ShapeDtypeStruct((total, width), BF),
        ),
        in_specs=[
            smem,
            smem,
            whole((rows, width)),
            whole((1, width)),
            whole((1, width)),
            col,
            col,
            col,
            pl.BlockSpec((quad, width), lambda j: (j, 0)),
            whole((1, width)),
            whole((1, width)),
            whole(pick_rows.shape),
            whole(slot_rows.shape),
        ],
        out_specs=(
            whole((rows, width)),
            seq,
            seq,
            seq,
            pl.BlockSpec((4, rows, rows), lambda j: (j, 0, 0)),
            seq,
            seq,
            whole((rows, width)),
            whole((total, width)),
        ),
        scratch_shapes=[pltpu.VMEM((rows, width), BF)],
        compiler_params=params(),
        cost_estimate=pl.CostEstimate(
            flops=flops, bytes_accessed=30 * 1024 * 1024, transcendentals=HEADS * rows * rows
        ),
        name="front",
    )(count, patch, tokens, g1, s1, wq, wk, wv, wo, g2, s2, pick_rows, slot_rows)


GELU_A = 0.7978845608028654
GELU_B = 0.044715


def expert_kernel(
    x_ref,
    c_ref,
    wi_own_ref,
    wi_far_ref,
    wo_own_ref,
    wo_far_ref,
    bi_ref,
    bo_ref,
    router_ref,
    hid_ref,
    gp_ref,
    gout_ref,
    out_ref,
    gin_ref,
    gbi_ref,
    gbo_ref,
    grouter_ref,
    acc_out,
    acc_gin,
    prob,
    *,
    rb,
    axis,
):
    f = pl.program_id(0)
    steps = pl.num_programs(0)
    total, width = x_ref.shape
    experts = router_ref.shape[1]
    mine = lax.broadcasted_iota(jnp.int32, (total, experts), 1) == lax.axis_index(axis)

    @pl.when(f == 0)
    def _():
        logits = mm(x_ref[...], router_ref[...])
        powers = jnp.exp(logits - jnp.max(logits, axis=-1, keepdims=True))
        probs = powers / jnp.sum(powers, axis=-1, keepdims=True)
        prob[...] = probs
        chosen = jnp.sum(jnp.where(mine, probs, 0.0), axis=-1, keepdims=True)
        grads = (chosen * c_ref[...].astype(F32)).astype(BF)
        gout_ref[...] = grads
        gbo_ref[...] = jnp.sum(grads.astype(F32), axis=0, keepdims=True)
        acc_out[...] = jnp.broadcast_to(bo_ref[...].astype(F32), (total, width))
        acc_gin[...] = jnp.zeros((total, width), F32)

    near = f < steps // 2
    wi = jnp.where(near, wi_own_ref[...], wi_far_ref[...])
    wo = jnp.where(near, wo_own_ref[...], wo_far_ref[...])
    bi = bi_ref[...].astype(F32)
    bias_sum = jnp.zeros(gbi_ref.shape, F32)
    for b in range(0, total, rb):
        sl = slice(b, b + rb)
        v = mm(x_ref[sl, :], wi) + bi
        gh = mm_nt(gout_ref[sl, :], wo)
        vv = v * v
        t = jnp.tanh(v * (GELU_A + (GELU_A * GELU_B) * vv))
        half = 0.5 + 0.5 * t
        hid = (v * half).astype(BF)
        slope = half + (half * (1.0 - t)) * (v * (GELU_A + (3.0 * GELU_A * GELU_B) * vv))
        gp = (gh * slope).astype(BF)
        hid_ref[sl, :] = hid
        gp_ref[sl, :] = gp
        bias_sum = bias_sum + jnp.sum(gp.astype(F32), axis=0, keepdims=True)
        acc_out[sl, :] += mm(hid, wo)
        acc_gin[sl, :] += mm_nt(gp, wi)
    gbi_ref[...] = bias_sum

    @pl.when(f == steps - 1)
    def _():
        probs = prob[...]
        chosen = jnp.sum(jnp.where(mine, probs, 0.0), axis=-1, keepdims=True)
        eo = acc_out[...].astype(BF).astype(F32)
        out_ref[...] = (chosen * eo).astype(BF)
        gc = jnp.sum(eo * c_ref[...].astype(F32), axis=-1, keepdims=True)
        gl = (gc * chosen) * (jnp.where(mine, 1.0, 0.0) - probs)
        router = router_ref[...].astype(F32)
        extra = lax.dot_general(
            gl, router, (((1,), (1,)), ((), ())), precision=lax.Precision.HIGHEST, preferred_element_type=F32
        )
        gin_ref[...] = (acc_gin[...] + extra).astype(BF)
        high = gl.astype(BF)
        low = (gl - high.astype(F32)).astype(BF)
        grouter_ref[...] = mm_tn(x_ref[...], high) + mm_tn(x_ref[...], low)


def expert_pass(x, c, wi_own, wi_far, wo_own, wo_far, bi, bo, router, axis):
    total, width = x.shape
    half = wi_own.shape[1]
    chunk = 512 if half % 512 == 0 else half
    per = half // chunk
    steps = 2 * per
    experts = router.shape[1]
    near = lambda f: jnp.minimum(f, per - 1)
    far = lambda f: jnp.maximum(f - per, 0)
    act = pl.BlockSpec((total, chunk), lambda f: (0, f))
    return pl.pallas_call(
        functools.partial(expert_kernel, rb=pack_step(total), axis=axis),
        grid=(steps,),
        out_shape=(
            jax.ShapeDtypeStruct((total, 2 * half), BF),
            jax.ShapeDtypeStruct((total, 2 * half), BF),
            jax.ShapeDtypeStruct((total, width), BF),
            jax.ShapeDtypeStruct((total, width), BF),
            jax.ShapeDtypeStruct((total, width), BF),
            jax.ShapeDtypeStruct((1, 2 * half), F32),
            jax.ShapeDtypeStruct((1, width), F32),
            jax.ShapeDtypeStruct((width, experts), F32),
        ),
        in_specs=[
            whole((total, width)),
            whole((total, width)),
            pl.BlockSpec((width, chunk), lambda f: (0, near(f))),
            pl.BlockSpec((width, chunk), lambda f: (0, far(f))),
            pl.BlockSpec((chunk, width), lambda f: (near(f), 0)),
            pl.BlockSpec((chunk, width), lambda f: (far(f), 0)),
            pl.BlockSpec((1, chunk), lambda f: (0, f)),
            whole((1, width)),
            whole((width, experts)),
        ],
        out_specs=(
            act,
            act,
            whole((total, width)),
            whole((total, width)),
            whole((total, width)),
            pl.BlockSpec((1, chunk), lambda f: (0, f)),
            whole((1, width)),
            whole((width, experts)),
        ),
        scratch_shapes=[
            pltpu.VMEM((total, width), F32),
            pltpu.VMEM((total, width), F32),
            pltpu.VMEM((total, experts), F32),
        ],
        compiler_params=params(),
        cost_estimate=pl.CostEstimate(
            flops=16 * total * width * half, bytes_accessed=40 * 1024 * 1024, transcendentals=2 * total * half
        ),
        name="expert_pass",
    )(x, c, wi_own, wi_far, wo_own, wo_far, bi, bo, router)


def weight_kernel(x_ref, hid_ref, g_ref, gp_ref, dwi_ref, dwo_ref):
    dwo_ref[...] = mm_tn(hid_ref[...], g_ref[...]).astype(BF)
    dwi_ref[...] = mm_tn(x_ref[...], gp_ref[...]).astype(BF)


def weight_pass(x, hid, g, gp, first):
    total, width = x.shape
    half = hid.shape[1] // 2
    chunk = 512 if half % 512 == 0 else half
    per = half // chunk
    act = pl.BlockSpec((total, chunk), lambda f: (0, f + first * per))
    return pl.pallas_call(
        weight_kernel,
        grid=(per,),
        out_shape=(
            jax.ShapeDtypeStruct((width, half), BF),
            jax.ShapeDtypeStruct((half, width), BF),
        ),
        in_specs=[whole((total, width)), act, whole((total, width)), act],
        out_specs=(
            pl.BlockSpec((width, chunk), lambda f: (0, f)),
            pl.BlockSpec((chunk, width), lambda f: (f, 0)),
        ),
        compiler_params=params(),
        cost_estimate=pl.CostEstimate(
            flops=4 * total * width * half, bytes_accessed=20 * 1024 * 1024, transcendentals=0
        ),
        name="weight_pass",
    )(x, hid, g, gp)


def live_rows(count, patch, rows):
    row = lax.broadcasted_iota(jnp.int32, (rows, 1), 0)
    return row < count * patch


def output_kernel(count_ref, patch_ref, pick_ref, slot_ref, back_ref, res_ref, out_ref, *, capacity):
    live = live_rows(count_ref[0], patch_ref[0], res_ref.shape[0])
    mixture = unpack_rows(back_ref, pick_ref[...], slot_ref[...], capacity)
    out_ref[...] = jnp.where(live, res_ref[...] + mixture, 0.0).astype(BF)


def output_pass(count, patch, picks, slots, back, res, capacity):
    rows, width = res.shape
    return pl.pallas_call(
        functools.partial(output_kernel, capacity=capacity),
        out_shape=jax.ShapeDtypeStruct((rows, width), BF),
        in_specs=[pl.BlockSpec(memory_space=SMEM)] * 2 + [pl.BlockSpec(memory_space=VM)] * 4,
        out_specs=pl.BlockSpec(memory_space=VM),
        compiler_params=params(),
        cost_estimate=pl.CostEstimate(
            flops=2 * back.shape[0] * rows * width, bytes_accessed=6 * 1024 * 1024, transcendentals=0
        ),
        name="output_pass",
    )(count, patch, picks, slots, back, res)


def middle_kernel(
    count_ref,
    patch_ref,
    pick_ref,
    slot_ref,
    back_ref,
    cot_ref,
    res_ref,
    gain2_ref,
    mixed_ref,
    wo_ref,
    gres_ref,
    gmix_ref,
    dwo_ref,
    ggain_ref,
    gshift_ref,
    *,
    capacity,
):
    live = live_rows(count_ref[0], patch_ref[0], res_ref.shape[0])
    gn = unpack_rows(back_ref, pick_ref[...], slot_ref[...], capacity)
    unit, inv = standardize(res_ref[...])
    ggain_ref[...] = jnp.sum(gn * unit, axis=0, keepdims=True)
    gshift_ref[...] = jnp.sum(gn, axis=0, keepdims=True)
    gout = jnp.where(live, cot_ref[...].astype(F32), 0.0)
    gres = gout + norm_back(gn, gain2_ref[...], unit, inv)
    gres_ref[...] = gres
    branch = gres.astype(BF)
    gmix_ref[...] = mm_nt(branch, wo_ref[...]).astype(BF)
    dwo_ref[...] = mm_tn(mixed_ref[...], branch).astype(BF)


def middle_pass(count, patch, picks, slots, back, cot, res, g2, mixed, wo, capacity):
    rows, width = res.shape
    vm = pl.BlockSpec(memory_space=VM)
    return pl.pallas_call(
        functools.partial(middle_kernel, capacity=capacity),
        out_shape=(
            jax.ShapeDtypeStruct((rows, width), F32),
            jax.ShapeDtypeStruct((rows, width), BF),
            jax.ShapeDtypeStruct((width, width), BF),
            jax.ShapeDtypeStruct((1, width), F32),
            jax.ShapeDtypeStruct((1, width), F32),
        ),
        in_specs=[pl.BlockSpec(memory_space=SMEM)] * 2 + [vm] * 8,
        out_specs=(vm,) * 5,
        compiler_params=params(),
        cost_estimate=pl.CostEstimate(
            flops=2 * rows * width * (back.shape[0] + 2 * width),
            bytes_accessed=14 * 1024 * 1024,
            transcendentals=0,
        ),
        name="middle_pass",
    )(count, patch, picks, slots, back, cot, res, g2, mixed, wo)


def attend_back_kernel(
    n1_ref,
    q_ref,
    k_ref,
    v_ref,
    p_ref,
    linv_ref,
    mixed_ref,
    gmix_ref,
    dq_ref,
    dk_ref,
    dv_ref,
    dwq_ref,
    dwk_ref,
    dwv_ref,
    ds_ref,
    *,
    head_dim,
    qb,
):
    rows, cols = q_ref.shape
    lane = lax.broadcasted_iota(jnp.int32, (rows, 2 * head_dim), 1)
    scale = jnp.asarray(head_dim ** (-0.5), BF)
    zero = jnp.zeros((rows, 2 * head_dim), BF)
    for pair in range(cols // (2 * head_dim)):
        sl = slice(pair * 2 * head_dim, (pair + 1) * 2 * head_dim)
        q_pair = q_ref[:, sl] * scale
        k_pair = k_ref[:, sl] * scale
        v_pair = v_ref[:, sl]
        do_pair = (gmix_ref[:, sl].astype(F32) * linv_ref[:, sl]).astype(BF)
        inner = do_pair.astype(F32) * mixed_ref[:, sl].astype(F32)
        dq = None
        for h in range(2):
            mine = (lane >= h * head_dim) & (lane < (h + 1) * head_dim)
            dom = jnp.where(mine, do_pair, zero)
            qm = jnp.where(mine, q_pair, zero)
            km = jnp.where(mine, k_pair, zero)
            row_inner = jnp.sum(jnp.where(mine, inner, 0.0), axis=-1, keepdims=True)
            head = pair * 2 + h
            for b in range(0, rows, qb):
                dp = mm_nt(dom[b : b + qb], v_pair)
                p = p_ref[head, b : b + qb, :].astype(F32)
                ds_ref[b : b + qb, :] = (p * (dp - row_inner[b : b + qb])).astype(BF)
            ds = ds_ref[...]
            dq_h = mm(ds, km)
            dk_h = mm_tn(ds, qm)
            dv_h = mm_tn(p_ref[head], dom)
            if h == 0:
                dq, dk, dv = dq_h, dk_h, dv_h
            else:
                dq, dk, dv = dq + dq_h, dk + dk_h, dv + dv_h
        dq_ref[:, sl] = dq.astype(BF)
        dk_ref[:, sl] = dk.astype(BF)
        dv_ref[:, sl] = dv.astype(BF)
    dwq_ref[...] = mm_tn(n1_ref[...], dq_ref[...]).astype(BF)
    dwk_ref[...] = mm_tn(n1_ref[...], dk_ref[...]).astype(BF)
    dwv_ref[...] = mm_tn(n1_ref[...], dv_ref[...]).astype(BF)


def attend_back(n1, q, k, v, p, linv, mixed, gmix):
    rows, width = n1.shape
    head_dim = width // HEADS
    quad = 4 * head_dim
    steps = width // quad
    seq = pl.BlockSpec((rows, quad), lambda j: (0, j))
    col = pl.BlockSpec((width, quad), lambda j: (0, j))
    return pl.pallas_call(
        functools.partial(attend_back_kernel, head_dim=head_dim, qb=rows // 5),
        grid=(steps,),
        out_shape=(jax.ShapeDtypeStruct((rows, width), BF),) * 3
        + (jax.ShapeDtypeStruct((width, width), BF),) * 3,
        in_specs=[
            whole((rows, width)),
            seq,
            seq,
            seq,
            pl.BlockSpec((4, rows, rows), lambda j: (j, 0, 0)),
            seq,
            seq,
            seq,
        ],
        out_specs=(seq, seq, seq, col, col, col),
        scratch_shapes=[pltpu.VMEM((rows, rows), BF)],
        compiler_params=params(),
        cost_estimate=pl.CostEstimate(
            flops=2 * rows * width * (3 * width + 4 * rows), bytes_accessed=24 * 1024 * 1024, transcendentals=0
        ),
        name="attend_back",
    )(n1, q, k, v, p, linv, mixed, gmix)


def tokens_kernel(
    dq_ref, dk_ref, dv_ref, wq_ref, wk_ref, wv_ref, tokens_ref, gain1_ref, gres_ref, gtok_ref, ggain_ref, gshift_ref
):
    gn = mm_nt(dq_ref[...], wq_ref[...]) + mm_nt(dk_ref[...], wk_ref[...]) + mm_nt(dv_ref[...], wv_ref[...])
    unit, inv = standardize(tokens_ref[...].astype(F32))
    ggain_ref[...] = jnp.sum(gn * unit, axis=0, keepdims=True)
    gshift_ref[...] = jnp.sum(gn, axis=0, keepdims=True)
    gtok_ref[...] = gres_ref[...] + norm_back(gn, gain1_ref[...], unit, inv)


def tokens_pass(dq, dk, dv, wq, wk, wv, tokens, g1, gres):
    rows, width = tokens.shape
    vm = pl.BlockSpec(memory_space=VM)
    return pl.pallas_call(
        tokens_kernel,
        out_shape=(
            jax.ShapeDtypeStruct((rows, width), F32),
            jax.ShapeDtypeStruct((1, width), F32),
            jax.ShapeDtypeStruct((1, width), F32),
        ),
        in_specs=[vm] * 9,
        out_specs=(vm,) * 3,
        compiler_params=params(),
        cost_estimate=pl.CostEstimate(
            flops=6 * rows * width * width, bytes_accessed=12 * 1024 * 1024, transcendentals=0
        ),
        name="tokens_pass",
    )(dq, dk, dv, wq, wk, wv, tokens, g1, gres)


def swap(value, axis, size, bit):
    return lax.ppermute(value, axis, [(i, i ^ bit) for i in range(size)])


def shards(
    tokens,
    cotangent,
    ln1_gain,
    ln1_shift,
    w_query,
    w_key,
    w_value,
    w_output,
    ln2_gain,
    ln2_shift,
    w_router,
    w_inner,
    b_inner,
    w_outer,
    b_outer,
    image_count,
    patches,
    picks,
    slots,
):
    rows, width = tokens.shape
    experts = w_router.shape[1]
    groups = lax.axis_size("expert")
    capacity = 21 * rows // (10 * experts)
    total = experts * capacity
    half = w_inner.shape[2]
    g1, s1 = ln1_gain[None, :], ln1_shift[None, :]
    g2, s2 = ln2_gain[None, :], ln2_shift[None, :]
    pick_rows, slot_rows = picks.T, slots.T

    def exchange(rows_out):
        return lax.all_to_all(
            rows_out.reshape(experts, capacity, width), "expert", split_axis=0, concat_axis=0, tiled=True
        ).reshape(total, width)

    cot_in = exchange(pack(pick_rows, slot_rows, cotangent, total, capacity))
    wi_own, wo_own = w_inner[0], w_outer[0]
    wi_far = swap(wi_own, "hidden", 2, 1)
    wo_far = swap(wo_own, "hidden", 2, 1)
    bi_all = jnp.concatenate([b_inner, swap(b_inner, "hidden", 2, 1)], axis=1)
    n1, q, k, v, p, linv, mixed, res, outgoing = front(
        image_count, patches, tokens, g1, s1, w_query, w_key, w_value, w_output, g2, s2,
        pick_rows, slot_rows, total, capacity,
    )
    x = exchange(outgoing)
    hid, gp, gout, out_rows, gin_rows, gbi, gbo, grouter = expert_pass(
        x, cot_in, wi_own, wi_far, wo_own, wo_far, bi_all, b_outer, w_router, "expert"
    )
    gin_back = exchange(gin_rows)
    dwi_far, dwo_far = weight_pass(x, hid, gout, gp, 1)
    dwi_own, dwo_own = weight_pass(x, hid, gout, gp, 0)
    out_back = exchange(out_rows)
    dwi = dwi_own.astype(F32) + swap(dwi_far, "hidden", 2, 1).astype(F32)
    dwo = dwo_own.astype(F32) + swap(dwo_far, "hidden", 2, 1).astype(F32)
    dwi = lax.psum(dwi.astype(BF), "dp").astype(F32)
    dwo = lax.psum(dwo.astype(BF), "dp").astype(F32)
    gbi = lax.psum(gbi[:, :half] + swap(gbi[:, half:], "hidden", 2, 1), "dp")
    gbo = lax.psum(gbo, ("hidden", "dp"))

    gres, gmix, dwout, ggain2, gshift2 = middle_pass(
        image_count, patches, picks, slots, gin_back, cotangent, res, g2, mixed, w_output, capacity
    )
    dq, dk, dv, dwq, dwk, dwv = attend_back(n1, q, k, v, p, linv, mixed, gmix)
    gtok, ggain1, gshift1 = tokens_pass(dq, dk, dv, w_query, w_key, w_value, tokens, g1, gres)
    block_out = output_pass(image_count, patches, picks, slots, out_back, res, capacity)
    everyone = ("expert", "hidden", "dp")
    dwq, dwk, dwv, dwout = lax.psum((dwq, dwk, dwv, dwout), everyone)
    ggain1, gshift1, ggain2, gshift2, grouter = lax.psum((ggain1, gshift1, ggain2, gshift2, grouter), everyone)
    return (
        block_out,
        gtok,
        ggain1[0],
        gshift1[0],
        dwq.astype(F32),
        dwk.astype(F32),
        dwv.astype(F32),
        dwout.astype(F32),
        ggain2[0],
        gshift2[0],
        grouter,
        dwi[None],
        gbi,
        dwo[None],
        gbo,
    )


def solution(mesh):
    rows = P(("expert", "hidden", "dp"), None)
    device = P(("expert", "hidden", "dp"))
    inner = P("expert", None, "hidden")
    inner_bias = P("expert", "hidden")
    outer = P("expert", "hidden", None)
    outer_bias = P("expert", None)
    return jax.shard_map(
        shards,
        mesh=mesh,
        in_specs=(rows, rows) + (P(),) * 9 + (inner, inner_bias, outer, outer_bias, device, device, rows, rows),
        out_specs=(rows, rows) + (P(),) * 9 + (inner, inner_bias, outer, outer_bias),
        check_vma=False,
    )
```

time: 798 us -> 562 us (0.70)
  matrix products: 161 us -> 0 us
  Pallas kernels: 0 us -> 141 us
  local copies, waits for them, and re-layouts: 99.3 us -> 9.83 us
  other arithmetic: 82.1 us -> 23.5 us
  waiting for transfers between devices: 312 us -> 272 us
  blocking collectives: 103 us -> 71.6 us
    dot_general x27 -> x0, matrix products: 161 us -> none  [the longest x1 19.5 us: shards(): jnp.einsum('erd,efd->erf', grad_inbound, outer_all, preferred_element_typ...]
    pallas_call x0 -> x9, Pallas kernels: none -> 141 us  [the longest x1 46.3 us: expert_pass(): pl.pallas_call(functools.partial(expert_kernel, rb=pack_step(total), axis...]
    all_to_all x1 -> x0, blocking collectives: 49.7 us -> none  [shards(): lax.all_to_all(pack_rows(grad_pair, dest_index, experts, capacity), 'expe...]
    reduce_sum x13 -> x0, other arithmetic: 32.9 us -> none  [the longest x1 11.9 us: shards(): jnp.sum(unpack_rows(grad_returned, dest_index, assigned_float), axis=1)]
    all_to_all x3 -> x4, waiting for transfers between devices: 118 us -> 91.9 us  [exchange(): lax.all_to_all(rows_out.reshape(experts, capacity, width), 'expert', spli...]
    gather x7 -> x0, local copies, waits for them, and re-layouts: 23.6 us -> none  [the longest x5 13.4 us: shards(): chosen = jnp.take_along_axis(gate_probs, picks, axis=1) * assigned_float]
    unnamed x166 -> x46, local copies, waits for them, and re-layouts: 29.8 us -> 7.5 us
    convert_element_type x9 -> x4, other arithmetic: 29.4 us -> 7.67 us  [the longest x1 2.94 us: shards(): dwq.astype(F32)]
  transfers between devices with their start and end apart: 10 -> 12, of which waited for: 5 -> 7; matrix products, arithmetic and copies ran while one was open for 32% -> 4% of each run, Pallas kernels for 0% -> 16%
where the time goes in v1:
time: 562 us; the launch traced here: 555 us
  waiting for transfers between devices  272 us (48%)
  Pallas kernels  141 us (25%)
  blocking collectives  71.6 us (13%)
  other arithmetic  23.5 us (4%)
  starting transfers between devices  20.1 us (4%)
  between operations  16 us (3%)
  local copies, waits for them, and re-layouts  9.83 us (2%)
    psum x1, waiting for transfers between devices, shards(): dwi = lax.psum(dwi.astype(BF), 'dp').astype(F32)  109 us
    all_to_all x4, waiting for transfers between devices, exchange(): lax.all_to_all(rows_out.reshape(experts, capacity, width), 'expert', spli...  91.9 us
    psum x1, waiting for transfers between devices, shards(): dwq, dwk, dwv, dwout = lax.psum((dwq, dwk, dwv, dwout), everyone)  65.5 us
    pallas_call x1, Pallas kernels, expert_pass(): pl.pallas_call(functools.partial(expert_kernel, rb=pack_step(total), axis...  46.3 us
    psum x1, blocking collectives, shards(): lax.psum((ggain1, gshift1, ggain2, gshift2, grouter), everyone)  46.3 us
    pallas_call x2, Pallas kernels, weight_pass(): pl.pallas_call(weight_kernel, grid=(per,), out_shape=(jax.ShapeDtypeStruc...  23.9 us
    pallas_call x1, Pallas kernels, front(): pl.pallas_call(functools.partial(front_kernel, capacity=capacity, head_di...  23.2 us
    pallas_call x1, Pallas kernels, attend_back(): pl.pallas_call(functools.partial(attend_back_kernel, head_dim=head_dim, q...  20.3 us
  transfers between devices with their start and end apart: 12, of which 7 were waited for; matrix products, arithmetic and copies ran while one was open for 4% of the time, Pallas kernels for 16%

profile of v1, /device:TPU:0, one launch (start us, length us, event | category | flops | bytes accessed | tf_op | source)
XLA Modules:
  0.0 554.7 jit_solution(7305558534118128801)
XLA Ops:
  7.2 4.3 pack_rows.1
  11.5 6.5 %all-to-all-start.1 = ((bf16[4,336,768]{2,1,0:T(8,128)(2,1)}), bf16[4,336,768]{2,1,0:T(8,128)(2,1)S(1)}, u32[]{:S(2)}, u32[]{:S(2)}) async-start(bf16[4,336,768]{2,1,0:T(8,128)(2,1)} %bitcast.24), calls=%async_computation.1 | async-start | bytes 4128768 | tf_op jit(solution)/shard_map/all_to_all | solution.py:669
  21.6 23.2 %front.1 = (bf16[640,768]{1,0:T(8,128)(2,1)}, bf16[640,768]{1,0:T(8,128)(2,1)}, bf16[640,768]{1,0:T(8,128)(2,1)}, bf16[640,768]{1,0:T(8,128)(2,1)}, bf16[12,640,...) custom-call(s32[1]{0:T(128)S(6)} %copy.46.count_ref, ...), custom_call_target="tpu_custom_call" | custom-call | flops 5599395840 | bytes 31457280 | tf_op jit(solution)/shard_map/front/pallas_call | solution.py:205
  44.9 20.6 %all-to-all-done.1 = bf16[4,336,768]{2,1,0:T(8,128)(2,1)S(1)} async-done(((bf16[4,336,768]{2,1,0:T(8,128)(2,1)}), bf16[4,336,768]{2,1,0:T(8,128)(2,1)S(1)}, u32[]{:S(2)}, u32[]{:S(2)}) %all-to-all-start.1) | async-done | bytes 2064416 | tf_op jit(solution)/shard_map/all_to_all | solution.py:669
  66.8 3.6 all-to-all-start
  71.9 3.1 collective-permute-done.2
  78.7 38.6 %all-to-all-done = bf16[4,336,768]{2,1,0:T(8,128)(2,1)S(1)} async-done(((bf16[4,336,768]{2,1,0:T(8,128)(2,1)}), bf16[4,336,768]{2,1,0:T(8,128)(2,1)S(1)}, u32[]{:S(2)}, u32[]{:S(2)}) %all-to-all-start) | async-done | bytes 2064416 | tf_op jit(solution)/shard_map/all_to_all | solution.py:669
  118.7 46.3 %expert_pass.1 = (bf16[1344,3072]{1,0:T(8,128)(2,1)}, bf16[1344,3072]{1,0:T(8,128)(2,1)}, bf16[1344,768]{1,0:T(8,128)(2,1)}, bf16[1344,768]{1,0:T(8,128)(2,1)}, ...) custom-call(bf16[1344,768]{1,0:T(8,128)(2,1)} %bitcast.18, ...), custom_call_target="tpu_custom_call" | custom-call | flops 25367150592 | bytes 41943040 | tf_op jit(solution)/shard_map/expert_pass/pallas_call | solution.py:352
  165.0 4.7 all-to-all-start.3
  169.8 11.9 %weight_pass.3 = (bf16[768,1536]{1,0:T(8,128)(2,1)}, bf16[1536,768]{1,0:T(8,128)(2,1)}) custom-call(bf16[1344,768]{1,0:T(8,128)(2,1)} %bitcast.19, bf16[1344,3072]{1,0:T(8,128)(2,1)} %get-tuple-element.76.hid_ref, bf16[1344,768]{1,0:T(8,128)(2,1)} %get-tuple-element.77.g_ref, bf16[1344,3072]{1,0:T(8,128)(2,1)} %get-tuple-element.78.gp_ref), custom_call_target="tpu_custom_call" | custom-call | flops 6341787648 | bytes 20971520 | tf_op jit(solution)/shard_map/weight_pass/pallas_call | solution.py:410
  184.1 32.7 %all-to-all-done.3 = bf16[4,336,768]{2,1,0:T(8,128)(2,1)} async-done(((bf16[4,336,768]{2,1,0:T(8,128)(2,1)}), bf16[4,336,768]{2,1,0:T(8,128)(2,1)}, u32[]{:S(2)}, u32[]{:S(2)}) %all-to-all-start.3) | async-done | bytes 2064416 | tf_op jit(solution)/shard_map/all_to_all | solution.py:669
  216.7 9.5 %middle_pass.1 = (f32[640,768]{1,0:T(8,128)}, bf16[640,768]{1,0:T(8,128)(2,1)}, bf16[768,768]{1,0:T(8,128)(2,1)}, f32[1,768]{1,0:T(1,128)}, f32[1,768]{1,0:T(1,128)}) custom-call(s32[1]{0:T(128)S(6)} %copy.46.count_ref, s32[1]{0:T(128)S(6)} %copy.47.patch_ref, s32[640,2]{1,0:T(8,128)} %copy.35.pick_ref, s32[640,2]{1,0:T(8,128)} %copy.36.slot_ref, ...), custom_call_target="tpu_custom_call" | custom-call | flops 2831155200 | bytes 14680064 | tf_op jit(solution)/shard_map/middle_pass/pallas_call | solution.py:491
  226.2 20.3 %attend_back.1 = (bf16[640,768]{1,0:T(8,128)(2,1)}, bf16[640,768]{1,0:T(8,128)(2,1)}, bf16[640,768]{1,0:T(8,128)(2,1)}, bf16[768,768]{1,0:T(8,128)(2,1)}, bf16[7...) custom-call(bf16[640,768]{1,0:T(8,128)(2,1)} %get-tuple-element.53.n1_ref, bf16[640,768]{1,0:T(8,128)(2,1)} %get-tuple-element.54.q_ref, ...), custom_call_target="tpu_custom_call" | custom-call | flops 4781506560 | bytes 25165824 | tf_op jit(solution)/shard_map/attend_back/pallas_call | solution.py:578
  246.9 11.9 %weight_pass.2 = (bf16[768,1536]{1,0:T(8,128)(2,1)}, bf16[1536,768]{1,0:T(8,128)(2,1)}) custom-call(bf16[1344,768]{1,0:T(8,128)(2,1)} %bitcast.20, bf16[1344,3072]{1,0:T(8,128)(2,1)} %get-tuple-element.76.hid_ref, bf16[1344,768]{1,0:T(8,128)(2,1)} %get-tuple-element.77.g_ref, bf16[1344,3072]{1,0:T(8,128)(2,1)} %get-tuple-element.78.gp_ref), custom_call_target="tpu_custom_call" | custom-call | flops 6341787648 | bytes 20971520 | tf_op jit(solution)/shard_map/weight_pass/pallas_call | solution.py:410
  258.8 4.6 fusion
  265.4 3.8 all-to-all-start.2
  269.3 15.6 %psum.103 = f32[1,768]{1,0:T(1,128)} all-reduce(f32[1,768]{1,0:T(1,128)S(1)} %copy-done.18), channel_id=1, replica_groups=mesh['expert'=4,'hidden'=2,'dp'=4] {'hidden','dp'}, use_global_device_ids=true, to_apply=%region_12.0 | all-reduce | flops 768 | bytes 6144 | tf_op jit(solution)/shard_map/psum | solution.py:695
  284.9 9.7 %psum.101 = f32[1,1536]{1,0:T(1,128)} all-reduce(f32[1,1536]{1,0:T(1,128)S(1)} %slice_add_fusion), channel_id=1, replica_groups=mesh['expert'=4,'hidden'=2,'dp'=4] {'dp'}, use_global_device_ids=true, to_apply=%region_10.0 | all-reduce | flops 1536 | bytes 12288 | tf_op jit(solution)/shard_map/psum | solution.py:694
  294.6 8.5 %tokens_pass.1 = (f32[640,768]{1,0:T(8,128)}, f32[1,768]{1,0:T(1,128)}, f32[1,768]{1,0:T(1,128)}) custom-call(bf16[640,768]{1,0:T(8,128)(2,1)} %get-tuple-element.62.dq_ref, bf16[640,768]{1,0:T(8,128)(2,1)} %get-tuple-element.63.dk_ref, bf16[640,768]{1,0:T(8,128)(2,1)} %get-tuple-element.64.dv_ref, bf16[768,768]{1,0:T(8,128)(2,1)} %wq_ref.3, ...), custom_call_target="tpu_custom_call" | custom-call | flops 2264924160 | bytes 12582912 | tf_op jit(solution)/shard_map/tokens_pass/pallas_call | solution.py:616
  304.6 46.3 %all-reduce = (f32[768]{0:T(1024)}, f32[768]{0:T(1024)}, f32[768]{0:T(1024)}, f32[768]{0:T(1024)}, f32[768,4]{1,0:T(8,128)S(1)}) all-reduce(f32[768]{0:T(1024)S(1)} %reduce, f32[768]{0:T(1024)S(1)} %reduce.1, f32[768]{0:T(1024)S(1)} %reduce.2, ...), channel_id=1, replica_groups=mesh['expert'=4,'hidden'=2,'dp'=4] {'expert','hidden','dp'}, use_global_device_ids=true, to_apply=%region_0.0 | all-reduce | flops 6144 | bytes 49152 | tf_op jit(solution)/shard_map/psum | solution.py:705
  352.9 5.3 output_pass.1
  358.2 65.5 %all-reduce.6.cloned.1.call-done = (bf16[768,768]{1,0:T(8,128)(2,1)}, bf16[768,768]{1,0:T(8,128)(2,1)}, bf16[768,768]{1,0:T(8,128)(2,1)}, bf16[768,768]{1,0:T(8,128)(2,1)}) async-done(((bf16[768,768]{1,0:T(8,128)(2,1)}, bf16[768,768]{1,0:T(8,128)(2,1)}, bf16[768,768]{1,0:T(8,128)(2,1)}, bf16[768,768]{1,0:T(8,128)(2,1)}), (bf16[768,768]{1,0:T(8,128)(2,1)}, bf16[768,768]{1,0:T(8,128)(2,1)}, ...) | async-done | bytes 4718608 | tf_op jit(solution)/shard_map/psum | solution.py:704
  431.5 108.7 %all-reduce.8.cloned.1.call-done = (bf16[1,768,1536]{2,1,0:T(8,128)(2,1)}, bf16[1,1536,768]{2,1,0:T(8,128)(2,1)}) async-done(((bf16[1,768,1536]{2,1,0:T(8,128)(2,1)}, bf16[1,1536,768]{2,1,0:T(8,128)(2,1)}), (bf16[1,768,1536]{2,1,0:T(8,128)(2,1)}, bf16[1,1536,768]{2,1,0:T(8,128)(2,1)})) %all-reduce.8.cloned.1.call-update) | async-done | bytes 4718608 | tf_op jit(solution)/shard_map/psum | solution.py:692
  540.2 4.6 broadcast_in_dim.29
  (79 shorter events, 28.8 us)
Async XLA Ops:
  11.5 7.8 %copy-start.14 = (f32[768]{0:T(1024)S(1)}, f32[768]{0:T(1024)}, u32[]{:S(2)}) copy-start(f32[768]{0:T(1024)} %param.21) | copy-start | bytes 9220
  11.5 8.4 %copy-start.15 = (f32[768]{0:T(1024)S(1)}, f32[768]{0:T(1024)}, u32[]{:S(2)}) copy-start(f32[768]{0:T(1024)} %param.27) | copy-start | bytes 9220
  11.5 9.0 %copy-start.16 = (f32[768]{0:T(1024)S(1)}, f32[768]{0:T(1024)}, u32[]{:S(2)}) copy-start(f32[768]{0:T(1024)} %param.22) | copy-start | bytes 9220
  11.5 9.5 %copy-start.17 = (f32[768]{0:T(1024)S(1)}, f32[768]{0:T(1024)}, u32[]{:S(2)}) copy-start(f32[768]{0:T(1024)} %param.28) | copy-start | bytes 9220
  11.5 54.0 %all-to-all-start.1 = ((bf16[4,336,768]{2,1,0:T(8,128)(2,1)}), bf16[4,336,768]{2,1,0:T(8,128)(2,1)S(1)}, u32[]{:S(2)}, u32[]{:S(2)}) async-start(bf16[4,336,768]{2,1,0:T(8,128)(2,1)} %bitcast.24), calls=%async_computation.1 | async-start | bytes 4128768 | tf_op jit(solution)/shard_map/all_to_all | solution.py:669
  44.9 26.1 %copy-start.11 = (bf16[1,1536]{1,0:T(2,128)(2,1)S(1)}, bf16[1,1536]{1,0:T(2,128)(2,1)}, u32[]{:S(2)}) copy-start(bf16[1,1536]{1,0:T(2,128)(2,1)} %param.31) | copy-start | bytes 9220
  44.9 26.2 %copy-start.10 = (bf16[768,4]{0,1:T(4,128)(2,1)S(1)}, bf16[768,4]{0,1:T(4,128)(2,1)}, u32[]{:S(2)}) copy-start(bf16[768,4]{0,1:T(4,128)(2,1)} %param.29) | copy-start | bytes 18436
  66.8 50.6 %all-to-all-start = ((bf16[4,336,768]{2,1,0:T(8,128)(2,1)}), bf16[4,336,768]{2,1,0:T(8,128)(2,1)S(1)}, u32[]{:S(2)}, u32[]{:S(2)}) async-start(bf16[4,336,768]{2,1,0:T(8,128)(2,1)} %bitcast.22), calls=%async_computation | async-start | bytes 4128768 | tf_op jit(solution)/shard_map/all_to_all | solution.py:669
  70.4 5.2 collective-permute-start
  70.5 8.2 %collective-permute-start.1 = (bf16[1536,768]{1,0:T(8,128)(2,1)}, bf16[1536,768]{1,0:T(8,128)(2,1)}, u32[]{:S(2)}, u32[]{:S(2)}) collective-permute-start(bf16[1536,768]{1,0:T(8,128)(2,1)} %bitcast.31), channel_id=1, source_target_pairs={{0,4},{4,0},{1,5},{5,1},{2,6},{6,2},{3,7},{7,3},{8,12},{12,8},{9,1... | collective-permute-start | bytes 7077896 | tf_op jit(solution)/shard_map/ppermute | solution.py:634
  71.0 4.0 collective-permute-start.2
  165.0 51.7 %all-to-all-start.3 = ((bf16[4,336,768]{2,1,0:T(8,128)(2,1)}), bf16[4,336,768]{2,1,0:T(8,128)(2,1)}, u32[]{:S(2)}, u32[]{:S(2)}) async-start(bf16[4,336,768]{2,1,0:T(8,128)(2,1)} %bitcast.23), calls=%async_computation.3 | async-start | bytes 4128768 | tf_op jit(solution)/shard_map/all_to_all | solution.py:669
  169.7 254.0 %all-reduce.6.cloned.1.call-start = ((), (), s32[]{:S(2)}) async-start(), calls=%async_computation.4 | async-start | bytes 9437184 | tf_op jit(solution)/shard_map/psum | solution.py:704
  169.7 12.0 %copy-start.12 = (s32[640,2]{0,1:T(2,128)S(1)}, s32[640,2]{0,1:T(2,128)}, u32[]{:S(2)}) copy-start(s32[640,2]{0,1:T(2,128)} %param.36) | copy-start | bytes 15364
  169.7 12.9 %copy-start.13 = (s32[640,2]{0,1:T(2,128)S(1)}, s32[640,2]{0,1:T(2,128)}, u32[]{:S(2)}) copy-start(s32[640,2]{0,1:T(2,128)} %param.37) | copy-start | bytes 15364
  181.7 77.1 %collective-permute-start.3 = (bf16[768,1536]{1,0:T(8,128)(2,1)}, bf16[768,1536]{1,0:T(8,128)(2,1)}, u32[]{:S(2)}, u32[]{:S(2)}) collective-permute-start(bf16[768,1536]{1,0:T(8,128)(2,1)} %get-tuple-element.80), channel_id=1, source_target_pairs={{0,4},{4,0},{1,5},{5,1},{2,6},{6,2},{3,7},{7,3},{8,12},{12,8},{9,1... | collective-permute-start | bytes 7077896 | tf_op jit(solution)/shard_map/ppermute | solution.py:634
  183.6 79.8 %collective-permute-start.5 = (bf16[1536,768]{1,0:T(8,128)(2,1)}, bf16[1536,768]{1,0:T(8,128)(2,1)S(1)}, u32[]{:S(2)}, u32[]{:S(2)}) collective-permute-start(bf16[1536,768]{1,0:T(8,128)(2,1)} %get-tuple-element.83), channel_id=1, source_target_pairs={{0,4},{4,0},{1,5},{5,1},{2,6},{6,2},{3,7},{7,3},{8,12},{12,8},{9,1... | collective-permute-start | bytes 7077896 | tf_op jit(solution)/shard_map/ppermute | solution.py:634
  246.6 293.6 %all-reduce.8.cloned.1.call-start = ((), (), s32[]{:S(2)}) async-start(), calls=%async_computation.5 | async-start | bytes 9437184 | tf_op jit(solution)/shard_map/psum | solution.py:692
  265.4 86.2 %all-to-all-start.2 = ((bf16[4,336,768]{2,1,0:T(8,128)(2,1)}), bf16[4,336,768]{2,1,0:T(8,128)(2,1)S(1)}, u32[]{:S(2)}, u32[]{:S(2)}) async-start(bf16[4,336,768]{2,1,0:T(8,128)(2,1)} %bitcast.17), calls=%async_computation.2 | async-start | bytes 4128768 | tf_op jit(solution)/shard_map/all_to_all | solution.py:669
  269.2 15.7 %collective-permute-start.4 = (f32[1,1536]{1,0:T(1,128)S(1)}, f32[1,1536]{1,0:T(1,128)S(1)}, u32[]{:S(2)}, u32[]{:S(2)}) collective-permute-start(f32[1,1536]{1,0:T(1,128)S(1)} %slice.7), channel_id=1, source_target_pairs={{0,4},{4,0},{1,5},{5,1},{2,6},{6,2},{3,7},{7,3},{8,12},{12,8},{9,1... | collective-permute-start | bytes 18440 | tf_op jit(solution)/shard_map/ppermute | solution.py:634
  294.6 9.9 %copy-start.20 = (f32[1,768]{1,0:T(1,128)S(1)}, f32[1,768]{1,0:T(1,128)}, u32[]{:S(2)}) copy-start(f32[1,768]{1,0:T(1,128)} %get-tuple-element.73) | copy-start | bytes 9220
  294.6 9.9 %copy-start.19 = (f32[1,768]{1,0:T(1,128)S(1)}, f32[1,768]{1,0:T(1,128)}, u32[]{:S(2)}) copy-start(f32[1,768]{1,0:T(1,128)} %get-tuple-element.74) | copy-start | bytes 9220
  294.6 9.9 %copy-start.8 = (f32[768,4]{1,0:T(8,128)S(1)}, f32[768,4]{1,0:T(8,128)}, u32[]{:S(2)}) copy-start(f32[768,4]{1,0:T(8,128)} %get-tuple-element.75) | copy-start | bytes 36868
  540.2 4.7 copy-start.1
  (9 other events, 22.5 us)
Sparse Core Ops, SparseCore 0:
  246.7 177.0 all-reduce.5
  428.2 111.9 all-reduce.7
